TPU v7x, 32 devices: a whole 2x2x4 slice. The times are simulated.
32 devices in a mesh: region: 16 (over z, y, x), blk: 2 (over core).
Axes of the slice: x: 2, y: 2, z: 4, core: 2. Of those that a mesh axis runs over, the one named last changes fastest.
Arguments:
- site_tensors: float32 [128, 2, 32, 1024], P('region', 'blk'), may hold values from -18 to 18
- projectors: bfloat16 [128, 2, 32, 1024], P('region'), may hold values from -0.1875 to 0.1875
- gate_matrix: float32 [2, 2, 2, 2], replicated, may hold values from -3 to 3
- recv_src: int32 [128, 3], P('region'), may hold values from 0 to 88, as said below
- cut_list: int32 [160], P('region'), may hold values from 0 to 23, as said below
- cut_dest: int32 [16, 10], replicated, may hold values from -1 to 63, as said below
- gate_src: int32 [128], P('region'), may hold values from 0 to 24, as said below
- gate_list: int32 [32], P('region'), may hold values from 0 to 7, as said below
- gate_dest: int32 [16, 2], replicated, may hold values from -1 to 15, as said below
Outputs:
- new_sites: float32 [128, 2, 32, 1024], P('region', 'blk')
- messages: float32 [128, 3, 1024], P('region')
Inputs may be any that keep to these rules, and one draw needn't show every extreme that they name: `recv_src`: messages between one ordered pair of regions use distinct slots below 4; some pair uses all 4. `cut_list`: entries whose cut_dest is -1 are padding. `cut_dest`: some region fills all 10 entries of its row. `gate_src`: gate partners form pairs along vertical links. `gate_list`: entries whose gate_dest is -1 are padding. `gate_dest`: some region fills all 2 entries of its row.
All inputs are finite; a program needn't handle non-finite values.
Results may differ from a plain program's by a relative error of at most 0.0039.
Values may be sent and summed in bfloat16 or wider, within the bound.
A program may use at most 128 MiB of HBM per device.

v0:
```python
import jax
import jax.numpy as jnp
from jax import lax
from jax.sharding import PartitionSpec as P

SWEEPS = 2
CAP = 4
GCAP = 1
HIGHEST = lax.Precision.HIGHEST
EPSILON = 1e-06


def weighted(tensors, incoming):
    partial_a = jnp.einsum("isabc,iag->isgbc", tensors, incoming[:, 0], precision=HIGHEST)
    return jnp.einsum("isgbc,ibe->isgec", partial_a, incoming[:, 1], precision=HIGHEST)


def outgoing(tensors, incoming):
    partial_c = jnp.einsum("isabc,icd->isabd", tensors, incoming[:, 2], precision=HIGHEST)
    both_bc = jnp.einsum("isabd,ibe->isaed", partial_c, incoming[:, 1], precision=HIGHEST)
    leg_zero = jnp.einsum("isaed,isfed->iaf", both_bc, tensors, precision=HIGHEST)
    both_ac = jnp.einsum("isabd,iag->isgbd", partial_c, incoming[:, 0], precision=HIGHEST)
    leg_one = jnp.einsum("isgbd,isghd->ibh", both_ac, tensors, precision=HIGHEST)
    both_ab = weighted(tensors, incoming)
    leg_two = jnp.einsum("isgec,isgek->ick", both_ab, tensors, precision=HIGHEST)
    return jnp.stack([leg_zero, leg_one, leg_two], axis=1)


def normalized(leg_terms):
    trace_sum = jnp.trace(leg_terms, axis1=2, axis2=3)
    return leg_terms.shape[-1] * leg_terms / trace_sum[:, :, None, None]


def select_rows(dest_table, my_region, capacity):
    region_count, columns = dest_table.shape
    wanted = my_region * capacity + jnp.arange(capacity, dtype=jnp.int32)
    matched = dest_table[:, :, None] == wanted[None, None, :]
    position = jnp.sum(
        jnp.where(matched, jnp.arange(columns, dtype=jnp.int32)[None, :, None], 0), axis=1
    )
    return (jnp.arange(region_count, dtype=jnp.int32)[:, None] * columns + position).reshape(-1)


def shards(
    site_tensors,
    projectors,
    gate_matrix,
    recv_src,
    cut_list,
    cut_dest,
    gate_src,
    gate_list,
    gate_dest,
):
    site_count = site_tensors.shape[0]
    bond_dim = site_tensors.shape[2]
    regions = lax.axis_size("region")
    my_region = lax.axis_index("region")
    my_spin = lax.axis_index("blk")
    tensors = site_tensors.reshape(site_count, 1, bond_dim, bond_dim, bond_dim)
    boundary = jnp.zeros((bond_dim, bond_dim), jnp.float32).at[0, 0].set(bond_dim)
    identity = jnp.eye(bond_dim, dtype=jnp.float32)
    msg_none = 3 * site_count + regions * CAP
    incoming = jnp.where((recv_src == msg_none)[:, :, None, None], boundary, identity)
    edge_row = boundary.reshape(1, bond_dim * bond_dim)
    for sweep_index in range(SWEEPS):
        totals = lax.psum(outgoing(tensors, incoming), "blk")
        fresh_msgs = normalized(totals).reshape(3 * site_count, bond_dim * bond_dim)
        leaving = fresh_msgs[cut_list]
        everyone = lax.all_gather(leaving, "region", axis=0, tiled=True)
        arrived = everyone[select_rows(cut_dest, my_region, CAP)]
        lookup = jnp.concatenate([fresh_msgs, arrived, edge_row], axis=0)
        incoming = lookup[recv_src].reshape(site_count, 3, bond_dim, bond_dim)
    messages = incoming.reshape(site_count, 3, bond_dim * bond_dim)
    weights = (
        weighted(tensors, incoming)
        .astype(jnp.bfloat16)
        .reshape(site_count, bond_dim * bond_dim, bond_dim)
    )
    factor = jnp.einsum(
        "ikc,isnk->icsn", weights, projectors, preferred_element_type=jnp.float32
    ).astype(jnp.bfloat16)
    factor = factor.reshape(site_count, 1, bond_dim, 2 * bond_dim)
    halves = lax.all_gather(factor, "blk", axis=1, tiled=True)
    flat_factor = halves.reshape(site_count, 4 * bond_dim * bond_dim)
    leaving_factor = flat_factor[gate_list]
    everyone_factor = lax.all_gather(leaving_factor, "region", axis=0, tiled=True)
    arrived_factor = everyone_factor[select_rows(gate_dest, my_region, GCAP)]
    empty_row = jnp.zeros((1, 4 * bond_dim * bond_dim), jnp.bfloat16)
    factor_lookup = jnp.concatenate([flat_factor, arrived_factor, empty_row], axis=0)
    partners = factor_lookup[gate_src].reshape(site_count, 2, bond_dim, 2, bond_dim)
    mixing = jnp.einsum(
        "ajby,iycjn->iabcn", gate_matrix, partners.astype(jnp.float32), precision=HIGHEST
    )
    own_old = lax.dynamic_index_in_dim(mixing, my_spin, 2, keepdims=False)
    spin_piece = jnp.einsum("iuvc,iacn->iauvn", tensors[:, 0], own_old, precision=HIGHEST)
    spin_piece = spin_piece.reshape(site_count, 2, bond_dim, bond_dim * bond_dim)
    summed = lax.psum_scatter(spin_piece, "blk", scatter_dimension=1, tiled=True)
    squares = jnp.sum(summed * summed, axis=(1, 2, 3))
    total_sq = lax.psum(squares, "blk")
    mean_sq = total_sq / (2 * bond_dim**3)
    updated = summed / jnp.sqrt(mean_sq + EPSILON)[:, None, None, None]
    unchanged = gate_src == site_count + regions * GCAP
    new_sites = jnp.where(unchanged[:, None, None, None], site_tensors, updated)
    return (new_sites, messages)


def solution(mesh):
    return jax.shard_map(
        shards,
        mesh=mesh,
        in_specs=(
            P("region", "blk", None, None),
            P("region", None, None, None),
            P(),
            P("region", None),
            P("region"),
            P(),
            P("region"),
            P("region"),
            P(),
        ),
        out_specs=(P("region", "blk", None, None), P("region", None, None)),
        check_vma=False,
    )
```

profile of v0, /device:TPU:0, one launch (start us, length us, event | category | flops | bytes accessed | tf_op | source)
XLA Modules:
  0.0 483.6 jit_solution(1316465474755128273)
XLA Ops:
  8.0 3.9 reshape.220
  11.9 6.4 %copy.94 = f32[8,32,32,32]{2,1,3,0:T(8,128)} copy(f32[8,32,32,32]{3,2,1,0:T(8,128)} %reshape.220) | data formatting | bytes 2097152 | tf_op jit(solution)/shard_map/reshape.47
  18.4 20.8 %convolution_bitcast_fusion.3 = f32[8,32,32,32]{2,3,1,0:T(8,128)S(1)} fusion(f32[8,32,32,32]{3,2,1,0:T(8,128)} %reshape.220, f32[8,3,32,32]{2,3,0,1:T(8,128)S(1)} %broadcast_select_fusion), kind=kOutput, calls=%fused_computation.35 | convolution fusion | flops 100663296 | bytes 2228224 | tf_op jit(solution)/shard_map/isabc,icd->isabd/dot_general | solution.py:19
  39.2 9.3 %fusion.14 = f32[8,32,32,32]{1,2,3,0:T(8,128)} fusion(f32[8,32,32,32]{2,3,1,0:T(8,128)S(1)} %convolution_bitcast_fusion.3, f32[8,3,32,32]{2,3,0,1:T(8,128)S(1)} %broadcast_select_fusion), kind=kOutput, calls=%fused_computation.23 | convolution fusion | flops 100663296 | bytes 5373952 | tf_op jit(solution)/shard_map/isabd,iag->isgbd/dot_general | solution.py:22
  48.5 20.6 %convolution_bitcast_fusion.2 = f32[8,32,32,32]{3,2,1,0:T(8,128)} fusion(f32[8,32,32,32]{2,3,1,0:T(8,128)S(1)} %convolution_bitcast_fusion.3, f32[8,3,32,32]{2,3,0,1:T(8,128)S(1)} %broadcast_select_fusion), kind=kOutput, calls=%fused_computation.34 | convolution fusion | flops 100663296 | bytes 5373952 | tf_op jit(solution)/shard_map/isabd,ibe->isaed/dot_general | solution.py:20
  69.1 6.8 %fusion.20 = f32[8,32,32,32]{3,1,2,0:T(8,128)} fusion(f32[8,32,32,32]{3,2,1,0:T(8,128)S(1)} %copy-done.1, f32[8,3,32,32]{2,3,0,1:T(8,128)S(1)} %broadcast_select_fusion), kind=kOutput, calls=%fused_computation.29 | convolution fusion | flops 100663296 | bytes 5373952 | tf_op jit(solution)/shard_map/isabc,iag->isgbc/dot_general | solution.py:14
  75.9 6.6 %copy.93 = f32[8,32,32,32]{2,1,3,0:T(8,128)} copy(f32[8,32,32,32]{3,2,1,0:T(8,128)} %convolution_bitcast_fusion.2) | data formatting | bytes 2097152 | tf_op jit(solution)/shard_map/reshape.51
  82.5 9.7 %convolution_bitcast_fusion.7 = f32[8,1,32,32]{3,2,0,1:T(8,128)S(1)} fusion(f32[8,32,32,32]{1,2,3,0:T(8,128)} %fusion.14, f32[8,32,32,32]{2,1,3,0:T(8,128)} %copy.94), kind=kOutput, calls=%fused_computation.43 | convolution fusion | flops 100663296 | bytes 2129920 | tf_op jit(solution)/shard_map/isgbd,isghd->ibh/dot_general | solution.py:23
  92.3 4.1 convolution_bitcast_fusion.8
  96.5 6.6 %fusion.12 = f32[8,32,32,32]{3,1,2,0:T(8,128)S(1)} fusion(f32[8,32,32,32]{3,1,2,0:T(8,128)S(1)} %copy-done.8, f32[8,3,32,32]{2,3,0,1:T(8,128)S(1)} %broadcast_select_fusion), kind=kOutput, calls=%fused_computation.21 | convolution fusion | flops 100663296 | bytes 5373952 | tf_op jit(solution)/shard_map/isgbc,ibe->isgec/dot_general | solution.py:15
  103.1 7.0 %fusion.28 = f32[8,1,32,32]{3,2,0,1:T(8,128)S(1)} fusion(f32[8,32,32,32]{3,2,1,0:T(8,128)S(1)} %copy-done.2, f32[8,32,32,32]{3,1,2,0:T(8,128)S(1)} %fusion.12), kind=kOutput, calls=%fused_computation.39 | convolution fusion | flops 100663296 | bytes 2129920 | tf_op jit(solution)/shard_map/isgec,isgek->ick/dot_general | solution.py:25
  114.8 17.5 %all-reduce.5.cloned.1.call-done = f32[8,3,32,32]{3,2,0,1:T(8,128)} async-done(((f32[8,3,32,32]{3,2,0,1:T(8,128)}), f32[8,3,32,32]{3,2,0,1:T(8,128)}) %all-reduce.5.cloned.1.call-update) | async-done | bytes 98320 | tf_op jit(solution)/shard_map/psum | solution.py:67
  135.3 49.6 %all-gather.3 = f32[16,10,1024]{2,1,0:T(8,128)} all-gather(f32[1,10,1024]{2,1,0:T(8,128)S(1)} %bitcast.197), channel_id=2, replica_groups=mesh['region'=16,'blk'=2] {'region'}, dimensions={0}, use_global_device_ids=true | all-gather | bytes 696320 | tf_op jit(solution)/shard_map/all_gather | solution.py:70
  187.8 21.2 %convolution_bitcast_fusion.1 = f32[8,32,32,32]{2,3,1,0:T(8,128)S(1)} fusion(f32[8,32,32,32]{3,2,1,0:T(8,128)} %reshape.220, f32[8,3,32,32]{3,2,1,0:T(8,128)S(1)} %reshape.224), kind=kOutput, calls=%fused_computation.33 | convolution fusion | flops 100663296 | bytes 2228224 | tf_op jit(solution)/shard_map/isabc,icd->isabd/dot_general | solution.py:19
  209.0 8.4 %fusion.10 = f32[8,32,32,32]{1,2,3,0:T(8,128)S(1)} fusion(f32[8,32,32,32]{2,3,1,0:T(8,128)S(1)} %convolution_bitcast_fusion.1, f32[8,3,32,32]{3,2,1,0:T(8,128)S(1)} %reshape.224), kind=kOutput, calls=%fused_computation.19 | convolution fusion | flops 100663296 | bytes 5373952 | tf_op jit(solution)/shard_map/isabd,iag->isgbd/dot_general | solution.py:22
  217.4 21.1 %convolution_bitcast_fusion = f32[8,32,32,32]{3,2,1,0:T(8,128)} fusion(f32[8,32,32,32]{2,3,1,0:T(8,128)S(1)} %convolution_bitcast_fusion.1, f32[8,3,32,32]{3,2,1,0:T(8,128)S(1)} %reshape.224), kind=kOutput, calls=%fused_computation.32 | convolution fusion | flops 100663296 | bytes 5373952 | tf_op jit(solution)/shard_map/isabd,ibe->isaed/dot_general | solution.py:20
  238.5 6.9 %fusion.18 = f32[8,32,32,32]{3,1,2,0:T(8,128)} fusion(f32[8,32,32,32]{3,2,1,0:T(8,128)S(1)} %copy-done.3, f32[8,3,32,32]{3,2,1,0:T(8,128)S(1)} %reshape.224), kind=kOutput, calls=%fused_computation.27 | convolution fusion | flops 100663296 | bytes 5373952 | tf_op jit(solution)/shard_map/isabc,iag->isgbc/dot_general | solution.py:14
  245.4 6.3 %convolution_bitcast_fusion.5 = f32[8,1,32,32]{3,2,0,1:T(8,128)S(1)} fusion(f32[8,32,32,32]{1,2,3,0:T(8,128)S(1)} %fusion.10, f32[8,32,32,32]{2,1,3,0:T(8,128)S(1)} %copy-done.6), kind=kOutput, calls=%fused_computation.41 | convolution fusion | flops 100663296 | bytes 2129920 | tf_op jit(solution)/shard_map/isgbd,isghd->ibh/dot_general | solution.py:23
  251.7 6.5 %copy.109 = f32[8,32,32,32]{2,1,3,0:T(8,128)} copy(f32[8,32,32,32]{3,2,1,0:T(8,128)} %convolution_bitcast_fusion) | data formatting | bytes 2097152 | tf_op jit(solution)/shard_map/reshape.70
  258.2 7.7 %convolution_bitcast_fusion.6 = f32[8,1,32,32]{3,2,0,1:T(8,128)S(1)} fusion(f32[8,32,32,32]{2,1,3,0:T(8,128)} %copy.109, f32[8,32,32,32]{2,1,3,0:T(8,128)} %copy.94), kind=kOutput, calls=%fused_computation.42 | convolution fusion | flops 100663296 | bytes 2129920 | tf_op jit(solution)/shard_map/isaed,isfed->iaf/dot_general | solution.py:21
  266.0 6.2 %fusion.8 = f32[8,32,32,32]{3,1,2,0:T(8,128)S(1)} fusion(f32[8,32,32,32]{3,1,2,0:T(8,128)S(1)} %copy-done.7, f32[8,3,32,32]{3,2,1,0:T(8,128)S(1)} %reshape.224), kind=kOutput, calls=%fused_computation.17 | convolution fusion | flops 100663296 | bytes 5373952 | tf_op jit(solution)/shard_map/isgbc,ibe->isgec/dot_general | solution.py:15
  272.2 7.2 %fusion.31 = f32[8,1,32,32]{3,2,0,1:T(8,128)S(1)} fusion(f32[8,32,32,32]{3,2,1,0:T(8,128)S(1)} %copy-done.4, f32[8,32,32,32]{3,1,2,0:T(8,128)S(1)} %fusion.8), kind=kOutput, calls=%fused_computation.40 | convolution fusion | flops 100663296 | bytes 2129920 | tf_op jit(solution)/shard_map/isgec,isgek->ick/dot_general | solution.py:25
  280.2 14.5 %all-reduce.7.cloned.1.call-done = f32[8,3,32,32]{3,2,0,1:T(8,128)} async-done(((f32[8,3,32,32]{3,2,0,1:T(8,128)}), f32[8,3,32,32]{3,2,0,1:T(8,128)}) %all-reduce.7.cloned.1.call-update) | async-done | bytes 98320 | tf_op jit(solution)/shard_map/psum | solution.py:67
  297.7 49.6 %all-gather.4 = f32[16,10,1024]{2,1,0:T(8,128)} all-gather(f32[1,10,1024]{2,1,0:T(8,128)S(1)} %bitcast.196), channel_id=3, replica_groups=mesh['region'=16,'blk'=2] {'region'}, dimensions={0}, use_global_device_ids=true | all-gather | bytes 696320 | tf_op jit(solution)/shard_map/all_gather | solution.py:70
  350.1 8.3 %fusion.16 = f32[8,32,32,32]{3,1,2,0:T(8,128)S(1)} fusion(f32[8,32,32,32]{3,2,1,0:T(8,128)} %reshape.220, f32[8,3,32,32]{3,2,1,0:T(8,128)S(1)} %reshape.228), kind=kOutput, calls=%fused_computation.25 | convolution fusion | flops 100663296 | bytes 2228224 | tf_op jit(solution)/shard_map/isabc,iag->isgbc/dot_general | solution.py:14
  358.5 5.6 %fusion.25 = bf16[8,32,32,32]{3,1,2,0:T(8,128)(2,1)S(1)} fusion(f32[8,32,32,32]{3,1,2,0:T(8,128)S(1)} %fusion.16, f32[8,3,32,32]{3,2,1,0:T(8,128)S(1)} %reshape.228), kind=kOutput, calls=%fused_computation.36 | convolution fusion | flops 100925440 | bytes 4849664 | tf_op jit(solution)/shard_map/isgbc,ibe->isgec/dot_general | solution.py:15
  368.2 37.0 %all-gather.5 = bf16[16,2,4096]{2,1,0:T(2,128)(2,1)S(1)} all-gather(bf16[1,2,4096]{2,1,0:T(2,128)(2,1)S(1)} %bitcast.198), channel_id=4, replica_groups=mesh['region'=16,'blk'=2] {'region'}, dimensions={0}, use_global_device_ids=true | all-gather | bytes 278528 | tf_op jit(solution)/shard_map/all_gather | solution.py:87
  408.2 24.5 %fusion.22 = f32[8,2,32,32,32]{3,4,2,1,0:T(8,128)} fusion(f32[8,32,32,32,1]{3,2,1,0,4:T(8,128)} %reshape.344, f32[8,2,32,32,1]{3,1,2,0,4:T(2,128)S(1)} %bitcast.195), kind=kOutput, calls=%fused_computation.31 | convolution fusion | flops 201326592 | bytes 3211264 | tf_op jit(solution)/shard_map/iuvc,iacn->iauvn/dot_general | solution.py:96
  432.7 9.0 %copy.129 = f32[8,2,32,32,32]{4,3,2,1,0:T(8,128)} copy(f32[8,2,32,32,32]{3,4,2,1,0:T(8,128)} %fusion.22) | data formatting | bytes 4194304 | tf_op jit(solution)/shard_map/iuvc,iacn->iauvn/transpose | solution.py:96
  441.6 7.7 %reshape.233 = f32[8,2,32,1024]{3,2,1,0:T(8,128)} reshape(f32[8,2,32,32,32]{4,3,2,1,0:T(8,128)} %copy.129) | data formatting | bytes 4194304 | tf_op jit(solution)/shard_map/reshape | solution.py:97
  450.0 18.5 %all-reduce.9.cloned.1.call-done = f32[8,2,32,1024]{3,2,1,0:T(8,128)} async-done(((f32[8,2,32,1024]{3,2,1,0:T(8,128)}), f32[8,2,32,1024]{3,2,1,0:T(8,128)}) %all-reduce.9.cloned.1.call-update) | async-done | bytes 2097168
  473.6 3.0 divide_select_fusion
  (121 shorter events, 30.7 us)
Async XLA Ops:
  7.2 356.9 %copy-start = (bf16[8,2,32,1024]{3,2,1,0:T(8,128)(2,1)S(1)}, bf16[8,2,32,1024]{3,2,1,0:T(8,128)(2,1)}, u32[]{:S(2)}) copy-start(bf16[8,2,32,1024]{3,2,1,0:T(8,128)(2,1)} %param.12) | copy-start | bytes 3145732
  7.2 125.1 %all-reduce.5.cloned.1.call-start = ((), (), s32[]{:S(2)}) async-start(), calls=%async_computation | async-start | bytes 786432 | tf_op jit(solution)/shard_map/psum | solution.py:67
  11.9 6.4 %copy-start.12 = (f32[32,32]{0,1:T(8,128)S(1)}, f32[32,32]{0,1:T(8,128)}, u32[]{:S(2)}) copy-start(f32[32,32]{0,1:T(8,128)} %constant.75.clone.1) | copy-start | bytes 12292
  48.5 20.6 %copy-start.1 = (f32[8,32,32,32]{3,2,1,0:T(8,128)S(1)}, f32[8,32,32,32]{3,2,1,0:T(8,128)}, u32[]{:S(2)}) copy-start(f32[8,32,32,32]{3,2,1,0:T(8,128)} %reshape.220) | copy-start | bytes 3145732
  82.5 9.8 %copy-start.5 = (f32[8,32,32,32]{2,1,3,0:T(8,128)S(1)}, f32[8,32,32,32]{2,1,3,0:T(8,128)}, u32[]{:S(2)}) copy-start(f32[8,32,32,32]{2,1,3,0:T(8,128)} %copy.94) | copy-start | bytes 3145732
  82.5 9.8 %copy-start.9 = (f32[8,32,32,32]{2,1,3,0:T(8,128)S(1)}, f32[8,32,32,32]{2,1,3,0:T(8,128)}, u32[]{:S(2)}) copy-start(f32[8,32,32,32]{2,1,3,0:T(8,128)} %copy.93) | copy-start | bytes 3145732
  92.3 4.1 copy-start.8
  96.4 6.6 %copy-start.2 = (f32[8,32,32,32]{3,2,1,0:T(8,128)S(1)}, f32[8,32,32,32]{3,2,1,0:T(8,128)}, u32[]{:S(2)}) copy-start(f32[8,32,32,32]{3,2,1,0:T(8,128)} %reshape.220) | copy-start | bytes 3145732
  103.1 7.9 %copy-start.13 = (s32[8,3]{0,1:T(4,128)S(1)}, s32[8,3]{0,1:T(4,128)}, u32[]{:S(2)}) copy-start(s32[8,3]{0,1:T(4,128)} %param.14) | copy-start | bytes 292
  103.1 8.0 %copy-start.10 = (f32[8,1,32,1024]{3,2,1,0:T(8,128)S(1)}, f32[8,1,32,1024]{3,2,1,0:T(8,128)}, u32[]{:S(2)}) copy-start(f32[8,1,32,1024]{3,2,1,0:T(8,128)} %param.11) | copy-start | bytes 3145732
  110.1 3.7 copy-start.16
  110.1 3.7 copy-start.17
  110.1 3.8 copy-start.18
  110.1 3.8 copy-start.19
  110.1 4.0 copy-start.15
  110.1 4.2 copy-start.14
  111.0 183.7 %all-reduce.7.cloned.1.call-start = ((), (), s32[]{:S(2)}) async-start(), calls=%async_computation.1 | async-start | bytes 786432 | tf_op jit(solution)/shard_map/psum | solution.py:67
  113.8 73.2 %copy-start.11 = (f32[1,1024]{1,0:T(1,128)S(1)}, f32[1,1024]{1,0:T(1,128)}, u32[]{:S(2)}) copy-start(f32[1,1024]{1,0:T(1,128)} %constant.84.clone.1) | copy-start | bytes 12292
  217.4 21.2 %copy-start.3 = (f32[8,32,32,32]{3,2,1,0:T(8,128)S(1)}, f32[8,32,32,32]{3,2,1,0:T(8,128)}, u32[]{:S(2)}) copy-start(f32[8,32,32,32]{3,2,1,0:T(8,128)} %reshape.220) | copy-start | bytes 3145732
  238.5 6.9 %copy-start.6 = (f32[8,32,32,32]{2,1,3,0:T(8,128)S(1)}, f32[8,32,32,32]{2,1,3,0:T(8,128)}, u32[]{:S(2)}) copy-start(f32[8,32,32,32]{2,1,3,0:T(8,128)} %copy.94) | copy-start | bytes 3145732
  258.2 7.7 %copy-start.7 = (f32[8,32,32,32]{3,1,2,0:T(8,128)S(1)}, f32[8,32,32,32]{3,1,2,0:T(8,128)}, u32[]{:S(2)}) copy-start(f32[8,32,32,32]{3,1,2,0:T(8,128)} %fusion.18) | copy-start | bytes 3145732
  266.0 6.2 %copy-start.4 = (f32[8,32,32,32]{3,2,1,0:T(8,128)S(1)}, f32[8,32,32,32]{3,2,1,0:T(8,128)}, u32[]{:S(2)}) copy-start(f32[8,32,32,32]{3,2,1,0:T(8,128)} %reshape.220) | copy-start | bytes 3145732
  280.2 188.3 %all-reduce.9.cloned.1.call-start = ((), (), s32[]{:S(2)}) async-start(), calls=%async_computation.2 | async-start | bytes 4194304
  441.6 7.7 %copy-start.20 = (u32[32]{0:T(128)S(1)}, u32[32]{0:T(128)}, u32[]{:S(2)}) copy-start(u32[32]{0:T(128)} %constant.101) | copy-start | bytes 388
Sparse Core Ops, SparseCore 0:
  111.1 21.1 all-reduce.4
  280.3 14.3 all-reduce.6
  449.5 19.0 all-reduce.8
where the time goes:
time: 492 us; the launch traced here: 484 us
  matrix products  210 us (43%)
  blocking collectives  141 us (29%)
  local copies, waits for them, and re-layouts  54.7 us (11%)
  waiting for transfers between devices  50.5 us (10%)
  between operations  14.8 us (3%)
  other arithmetic  12.3 us (2%)
    all_gather x2, blocking collectives, shards(): everyone = lax.all_gather(leaving, 'region', axis=0, tiled=True)  99.2 us
    dot_general x2, matrix products, outgoing(): jnp.einsum('isabc,icd->isabd', tensors, incoming[:, 2], precision=HIGHEST)  42 us
    dot_general x2, matrix products, outgoing(): jnp.einsum('isabd,ibe->isaed', partial_c, incoming[:, 1], precision=HIGHEST)  41.8 us
    all_gather x1, blocking collectives, shards(): lax.all_gather(leaving_factor, 'region', axis=0, tiled=True)  37 us
    psum x2, waiting for transfers between devices, shards(): totals = lax.psum(outgoing(tensors, incoming), 'blk')  32 us
    another operation x6, local copies, waits for them, and re-layouts  26.4 us
    dot_general x1, matrix products, shards(): jnp.einsum('iuvc,iacn->iauvn', tensors[:, 0], own_old, precision=HIGHEST)  24.5 us
    dot_general x3, matrix products, weighted(): jnp.einsum('isabc,iag->isgbc', tensors, incoming[:, 0], precision=HIGHEST)  22.1 us
  transfers between devices with their start and end apart: 3, of which 3 were waited for; matrix products, arithmetic and copies ran while one was open for 1% of the time, Pallas kernels for 0%

commit v1 on v0

--- a/solution.py
+++ b/solution.py
@@ -84,7 +84,32 @@
     halves = lax.all_gather(factor, "blk", axis=1, tiled=True)
     flat_factor = halves.reshape(site_count, 4 * bond_dim * bond_dim)
     leaving_factor = flat_factor[gate_list]
-    everyone_factor = lax.all_gather(leaving_factor, "region", axis=0, tiled=True)
+    block_next = lax.axis_index("region")
+    v_now = lax.axis_size("region")
+    arrivals = []
+    newest, passed, odd = (v_now, block_next, leaving_factor.shape[0])
+    for it, rr in enumerate(leaving_factor.shape):
+        arrivals.append(rr * newest if it == 0 else rr)
+    everyone_factor = lax.dynamic_update_slice_in_dim(
+        jnp.zeros(arrivals, leaving_factor.dtype), leaving_factor, passed * odd, axis=0
+    )
+    state_next = val2 = leaving_factor
+    for tick in range(1, newest // 2 + 1):
+        frames = []
+        for it in range(newest):
+            frames.append((it, (it + 1) % newest))
+        state_next = lax.ppermute(state_next, "region", perm=frames)
+        everyone_factor = lax.dynamic_update_slice_in_dim(
+            everyone_factor, state_next, (passed - tick) % newest * odd, axis=0
+        )
+        if 2 * tick < newest:
+            leaves = []
+            for it in range(newest):
+                leaves.append((it, (it - 1) % newest))
+            val2 = lax.ppermute(val2, "region", perm=leaves)
+            everyone_factor = lax.dynamic_update_slice_in_dim(
+                everyone_factor, val2, (passed + tick) % newest * odd, axis=0
+            )
     arrived_factor = everyone_factor[select_rows(gate_dest, my_region, GCAP)]
     empty_row = jnp.zeros((1, 4 * bond_dim * bond_dim), jnp.bfloat16)
     factor_lookup = jnp.concatenate([flat_factor, arrived_factor, empty_row], axis=0)

time: 492 us -> 512 us (1.041)
  starting transfers between devices: 0.12 us -> 39.7 us
  blocking collectives: 141 us -> 104 us
  waiting for transfers between devices: 50.5 us -> 67 us
    ppermute x0 -> x15, starting transfers between devices: none -> 39.6 us  [the longest x7 39.3 us: shards(): val2 = lax.ppermute(val2, 'region', perm=leaves)]
    all_gather x1 -> x0, blocking collectives: 37 us -> none  [shards(): lax.all_gather(leaving_factor, 'region', axis=0, tiled=True)]
    ppermute x0 -> x15, waiting for transfers between devices: none -> 18.8 us  [the longest x8 18.8 us: shards(): state_next = lax.ppermute(state_next, 'region', perm=frames)]
  transfers between devices with their start and end apart: 3 -> 18, of which waited for: 3 -> 11; matrix products, arithmetic and copies ran while one was open for 1% -> 1% of each run, Pallas kernels for 0% -> 0%
where the time goes in v1:
time: 512 us; the launch traced here: 503 us
  matrix products  210 us (41%)
  blocking collectives  104 us (20%)
  waiting for transfers between devices  67 us (13%)
  local copies, waits for them, and re-layouts  55.7 us (11%)
  starting transfers between devices  39.7 us (8%)
  between operations  15.2 us (3%)
  other arithmetic  12.4 us (2%)
    all_gather x2, blocking collectives, shards(): everyone = lax.all_gather(leaving, 'region', axis=0, tiled=True)  99.2 us
    dot_general x2, matrix products, outgoing(): jnp.einsum('isabc,icd->isabd', tensors, incoming[:, 2], precision=HIGHEST)  42.2 us
    dot_general x2, matrix products, outgoing(): jnp.einsum('isabd,ibe->isaed', partial_c, incoming[:, 1], precision=HIGHEST)  41.6 us
    ppermute x7, starting transfers between devices, shards(): val2 = lax.ppermute(val2, 'region', perm=leaves)  39.3 us
    psum x2, waiting for transfers between devices, shards(): totals = lax.psum(outgoing(tensors, incoming), 'blk')  31.6 us
    another operation x6, local copies, waits for them, and re-layouts  27 us
    dot_general x1, matrix products, shards(): jnp.einsum('iuvc,iacn->iauvn', tensors[:, 0], own_old, precision=HIGHEST)  24.5 us
    dot_general x3, matrix products, weighted(): jnp.einsum('isabc,iag->isgbc', tensors, incoming[:, 0], precision=HIGHEST)  22.1 us
  transfers between devices with their start and end apart: 18, of which 11 were waited for; matrix products, arithmetic and copies ran while one was open for 1% of the time, Pallas kernels for 0%

profile of v1, /device:TPU:0, one launch (start us, length us, event | category | flops | bytes accessed | tf_op | source)
XLA Modules:
  0.0 503.5 jit_solution(2931855762606209351)
XLA Ops:
  11.9 6.4 %copy.94 = f32[8,32,32,32]{2,1,3,0:T(8,128)} copy(f32[8,32,32,32]{3,2,1,0:T(8,128)} %reshape.220) | data formatting | bytes 2097152 | tf_op jit(solution)/shard_map/reshape.47
  18.5 20.8 %convolution_bitcast_fusion.3 = f32[8,32,32,32]{2,3,1,0:T(8,128)S(1)} fusion(f32[8,32,32,32]{3,2,1,0:T(8,128)} %reshape.220, f32[8,3,32,32]{2,3,0,1:T(8,128)S(1)} %broadcast_select_fusion), kind=kOutput, calls=%fused_computation.35 | convolution fusion | flops 100663296 | bytes 2228224 | tf_op jit(solution)/shard_map/isabc,icd->isabd/dot_general | solution.py:19
  39.2 9.3 %fusion.14 = f32[8,32,32,32]{1,2,3,0:T(8,128)} fusion(f32[8,32,32,32]{2,3,1,0:T(8,128)S(1)} %convolution_bitcast_fusion.3, f32[8,3,32,32]{2,3,0,1:T(8,128)S(1)} %broadcast_select_fusion), kind=kOutput, calls=%fused_computation.23 | convolution fusion | flops 100663296 | bytes 5373952 | tf_op jit(solution)/shard_map/isabd,iag->isgbd/dot_general | solution.py:22
  48.5 20.7 %convolution_bitcast_fusion.2 = f32[8,32,32,32]{3,2,1,0:T(8,128)} fusion(f32[8,32,32,32]{2,3,1,0:T(8,128)S(1)} %convolution_bitcast_fusion.3, f32[8,3,32,32]{2,3,0,1:T(8,128)S(1)} %broadcast_select_fusion), kind=kOutput, calls=%fused_computation.34 | convolution fusion | flops 100663296 | bytes 5373952 | tf_op jit(solution)/shard_map/isabd,ibe->isaed/dot_general | solution.py:20
  69.2 6.8 %fusion.20 = f32[8,32,32,32]{3,1,2,0:T(8,128)} fusion(f32[8,32,32,32]{3,2,1,0:T(8,128)S(1)} %copy-done.1, f32[8,3,32,32]{2,3,0,1:T(8,128)S(1)} %broadcast_select_fusion), kind=kOutput, calls=%fused_computation.29 | convolution fusion | flops 100663296 | bytes 5373952 | tf_op jit(solution)/shard_map/isabc,iag->isgbc/dot_general | solution.py:14
  76.1 6.8 %copy.93 = f32[8,32,32,32]{2,1,3,0:T(8,128)} copy(f32[8,32,32,32]{3,2,1,0:T(8,128)} %convolution_bitcast_fusion.2) | data formatting | bytes 2097152 | tf_op jit(solution)/shard_map/reshape.51
  82.9 9.7 %convolution_bitcast_fusion.7 = f32[8,1,32,32]{3,2,0,1:T(8,128)S(1)} fusion(f32[8,32,32,32]{1,2,3,0:T(8,128)} %fusion.14, f32[8,32,32,32]{2,1,3,0:T(8,128)} %copy.94), kind=kOutput, calls=%fused_computation.43 | convolution fusion | flops 100663296 | bytes 2129920 | tf_op jit(solution)/shard_map/isgbd,isghd->ibh/dot_general | solution.py:23
  96.8 6.3 %fusion.12 = f32[8,32,32,32]{3,1,2,0:T(8,128)S(1)} fusion(f32[8,32,32,32]{3,1,2,0:T(8,128)S(1)} %copy-done.8, f32[8,3,32,32]{2,3,0,1:T(8,128)S(1)} %broadcast_select_fusion), kind=kOutput, calls=%fused_computation.21 | convolution fusion | flops 100663296 | bytes 5373952 | tf_op jit(solution)/shard_map/isgbc,ibe->isgec/dot_general | solution.py:15
  103.2 7.0 %fusion.28 = f32[8,1,32,32]{3,2,0,1:T(8,128)S(1)} fusion(f32[8,32,32,32]{3,2,1,0:T(8,128)S(1)} %copy-done.2, f32[8,32,32,32]{3,1,2,0:T(8,128)S(1)} %fusion.12), kind=kOutput, calls=%fused_computation.39 | convolution fusion | flops 100663296 | bytes 2129920 | tf_op jit(solution)/shard_map/isgec,isgek->ick/dot_general | solution.py:25
  115.2 17.2 %all-reduce.5.cloned.1.call-done = f32[8,3,32,32]{3,2,0,1:T(8,128)} async-done(((f32[8,3,32,32]{3,2,0,1:T(8,128)}), f32[8,3,32,32]{3,2,0,1:T(8,128)}) %all-reduce.5.cloned.1.call-update) | async-done | bytes 98320 | tf_op jit(solution)/shard_map/psum | solution.py:67
  135.4 49.6 %all-gather.2 = f32[16,10,1024]{2,1,0:T(8,128)} all-gather(f32[1,10,1024]{2,1,0:T(8,128)S(1)} %bitcast.196), channel_id=2, replica_groups=mesh['region'=16,'blk'=2] {'region'}, dimensions={0}, use_global_device_ids=true | all-gather | bytes 696320 | tf_op jit(solution)/shard_map/all_gather | solution.py:70
  187.8 21.4 %convolution_bitcast_fusion.1 = f32[8,32,32,32]{2,3,1,0:T(8,128)S(1)} fusion(f32[8,32,32,32]{3,2,1,0:T(8,128)} %reshape.220, f32[8,3,32,32]{3,2,1,0:T(8,128)S(1)} %reshape.224), kind=kOutput, calls=%fused_computation.33 | convolution fusion | flops 100663296 | bytes 2228224 | tf_op jit(solution)/shard_map/isabc,icd->isabd/dot_general | solution.py:19
  209.3 8.4 %fusion.10 = f32[8,32,32,32]{1,2,3,0:T(8,128)S(1)} fusion(f32[8,32,32,32]{2,3,1,0:T(8,128)S(1)} %convolution_bitcast_fusion.1, f32[8,3,32,32]{3,2,1,0:T(8,128)S(1)} %reshape.224), kind=kOutput, calls=%fused_computation.19 | convolution fusion | flops 100663296 | bytes 5373952 | tf_op jit(solution)/shard_map/isabd,iag->isgbd/dot_general | solution.py:22
  217.7 20.9 %convolution_bitcast_fusion = f32[8,32,32,32]{3,2,1,0:T(8,128)} fusion(f32[8,32,32,32]{2,3,1,0:T(8,128)S(1)} %convolution_bitcast_fusion.1, f32[8,3,32,32]{3,2,1,0:T(8,128)S(1)} %reshape.224), kind=kOutput, calls=%fused_computation.32 | convolution fusion | flops 100663296 | bytes 5373952 | tf_op jit(solution)/shard_map/isabd,ibe->isaed/dot_general | solution.py:20
  238.6 6.9 %fusion.18 = f32[8,32,32,32]{3,1,2,0:T(8,128)} fusion(f32[8,32,32,32]{3,2,1,0:T(8,128)S(1)} %copy-done.3, f32[8,3,32,32]{3,2,1,0:T(8,128)S(1)} %reshape.224), kind=kOutput, calls=%fused_computation.27 | convolution fusion | flops 100663296 | bytes 5373952 | tf_op jit(solution)/shard_map/isabc,iag->isgbc/dot_general | solution.py:14
  245.5 6.0 %convolution_bitcast_fusion.5 = f32[8,1,32,32]{3,2,0,1:T(8,128)S(1)} fusion(f32[8,32,32,32]{1,2,3,0:T(8,128)S(1)} %fusion.10, f32[8,32,32,32]{2,1,3,0:T(8,128)S(1)} %copy-done.6), kind=kOutput, calls=%fused_computation.41 | convolution fusion | flops 100663296 | bytes 2129920 | tf_op jit(solution)/shard_map/isgbd,isghd->ibh/dot_general | solution.py:23
  251.5 6.8 %copy.109 = f32[8,32,32,32]{2,1,3,0:T(8,128)} copy(f32[8,32,32,32]{3,2,1,0:T(8,128)} %convolution_bitcast_fusion) | data formatting | bytes 2097152 | tf_op jit(solution)/shard_map/reshape.70
  258.3 7.7 %convolution_bitcast_fusion.6 = f32[8,1,32,32]{3,2,0,1:T(8,128)S(1)} fusion(f32[8,32,32,32]{2,1,3,0:T(8,128)} %copy.109, f32[8,32,32,32]{2,1,3,0:T(8,128)} %copy.94), kind=kOutput, calls=%fused_computation.42 | convolution fusion | flops 100663296 | bytes 2129920 | tf_op jit(solution)/shard_map/isaed,isfed->iaf/dot_general | solution.py:21
  266.0 6.2 %fusion.8 = f32[8,32,32,32]{3,1,2,0:T(8,128)S(1)} fusion(f32[8,32,32,32]{3,1,2,0:T(8,128)S(1)} %copy-done.7, f32[8,3,32,32]{3,2,1,0:T(8,128)S(1)} %reshape.224), kind=kOutput, calls=%fused_computation.17 | convolution fusion | flops 100663296 | bytes 5373952 | tf_op jit(solution)/shard_map/isgbc,ibe->isgec/dot_general | solution.py:15
  272.2 7.1 %fusion.31 = f32[8,1,32,32]{3,2,0,1:T(8,128)S(1)} fusion(f32[8,32,32,32]{3,2,1,0:T(8,128)S(1)} %copy-done.4, f32[8,32,32,32]{3,1,2,0:T(8,128)S(1)} %fusion.8), kind=kOutput, calls=%fused_computation.40 | convolution fusion | flops 100663296 | bytes 2129920 | tf_op jit(solution)/shard_map/isgec,isgek->ick/dot_general | solution.py:25
  280.3 14.4 %all-reduce.7.cloned.1.call-done = f32[8,3,32,32]{3,2,0,1:T(8,128)} async-done(((f32[8,3,32,32]{3,2,0,1:T(8,128)}), f32[8,3,32,32]{3,2,0,1:T(8,128)}) %all-reduce.7.cloned.1.call-update) | async-done | bytes 98320 | tf_op jit(solution)/shard_map/psum | solution.py:67
  297.7 49.6 %all-gather.3 = f32[16,10,1024]{2,1,0:T(8,128)} all-gather(f32[1,10,1024]{2,1,0:T(8,128)S(1)} %bitcast.195), channel_id=3, replica_groups=mesh['region'=16,'blk'=2] {'region'}, dimensions={0}, use_global_device_ids=true | all-gather | bytes 696320 | tf_op jit(solution)/shard_map/all_gather | solution.py:70
  350.1 8.3 %fusion.16 = f32[8,32,32,32]{3,1,2,0:T(8,128)S(1)} fusion(f32[8,32,32,32]{3,2,1,0:T(8,128)} %reshape.220, f32[8,3,32,32]{3,2,1,0:T(8,128)S(1)} %reshape.228), kind=kOutput, calls=%fused_computation.25 | convolution fusion | flops 100663296 | bytes 2228224 | tf_op jit(solution)/shard_map/isabc,iag->isgbc/dot_general | solution.py:14
  358.5 5.6 %fusion.25 = bf16[8,32,32,32]{3,1,2,0:T(8,128)(2,1)S(1)} fusion(f32[8,32,32,32]{3,1,2,0:T(8,128)S(1)} %fusion.16, f32[8,3,32,32]{3,2,1,0:T(8,128)S(1)} %reshape.228), kind=kOutput, calls=%fused_computation.36 | convolution fusion | flops 100925440 | bytes 4849664 | tf_op jit(solution)/shard_map/isgbc,ibe->isgec/dot_general | solution.py:15
  375.6 5.6 %collective-permute-start.3 = (bf16[2,4096]{1,0:T(2,128)(2,1)S(1)}, bf16[2,4096]{1,0:T(2,128)(2,1)S(1)}, u32[]{:S(2)}, u32[]{:S(2)}) collective-permute-start(bf16[2,4096]{1,0:T(2,128)(2,1)S(1)} %collective-permute-done.1), channel_id=1, source_target_pairs={{0,30},{2,0},{4,2},{6,4},{8,6},{10,8},{12,10},{14,12},{16,14},{18,... | collective-permute-start | bytes 49160 | tf_op jit(solution)/shard_map/ppermute | solution.py:109
  382.9 5.6 %collective-permute-start.5 = (bf16[2,4096]{1,0:T(2,128)(2,1)S(1)}, bf16[2,4096]{1,0:T(2,128)(2,1)S(1)}, u32[]{:S(2)}, u32[]{:S(2)}) collective-permute-start(bf16[2,4096]{1,0:T(2,128)(2,1)S(1)} %collective-permute-done.3), channel_id=1, source_target_pairs={{0,30},{2,0},{4,2},{6,4},{8,6},{10,8},{12,10},{14,12},{16,14},{18,... | collective-permute-start | bytes 49160 | tf_op jit(solution)/shard_map/ppermute | solution.py:109
  404.9 5.6 %collective-permute-start.11 = (bf16[2,4096]{1,0:T(2,128)(2,1)S(1)}, bf16[2,4096]{1,0:T(2,128)(2,1)S(1)}, u32[]{:S(2)}, u32[]{:S(2)}) collective-permute-start(bf16[2,4096]{1,0:T(2,128)(2,1)S(1)} %collective-permute-done.9), channel_id=1, source_target_pairs={{0,30},{2,0},{4,2},{6,4},{8,6},{10,8},{12,10},{14,12},{16,14},{18,... | collective-permute-start | bytes 49160 | tf_op jit(solution)/shard_map/ppermute | solution.py:109
  419.6 7.3 %collective-permute-done.14 = bf16[2,4096]{1,0:T(2,128)(2,1)S(1)} collective-permute-done((bf16[2,4096]{1,0:T(2,128)(2,1)S(1)}, bf16[2,4096]{1,0:T(2,128)(2,1)S(1)}, u32[]{:S(2)}, u32[]{:S(2)}) %collective-permute-start.14) | collective-permute-done | bytes 16416 | tf_op jit(solution)/shard_map/ppermute | solution.py:101
  429.8 24.5 %fusion.22 = f32[8,2,32,32,32]{3,4,2,1,0:T(8,128)} fusion(f32[8,32,32,32,1]{3,2,1,0,4:T(8,128)} %reshape.341, f32[8,2,32,32,1]{3,1,2,0,4:T(2,128)S(1)} %bitcast.194), kind=kOutput, calls=%fused_computation.31 | convolution fusion | flops 201326592 | bytes 3211264 | tf_op jit(solution)/shard_map/iuvc,iacn->iauvn/dot_general | solution.py:121
  454.4 9.0 %copy.129 = f32[8,2,32,32,32]{4,3,2,1,0:T(8,128)} copy(f32[8,2,32,32,32]{3,4,2,1,0:T(8,128)} %fusion.22) | data formatting | bytes 4194304 | tf_op jit(solution)/shard_map/iuvc,iacn->iauvn/transpose | solution.py:121
  463.3 7.7 %reshape.233 = f32[8,2,32,1024]{3,2,1,0:T(8,128)} reshape(f32[8,2,32,32,32]{4,3,2,1,0:T(8,128)} %copy.129) | data formatting | bytes 4194304 | tf_op jit(solution)/shard_map/reshape | solution.py:122
  471.7 16.6 %all-reduce.9.cloned.1.call-done = f32[8,2,32,1024]{3,2,1,0:T(8,128)} async-done(((f32[8,2,32,1024]{3,2,1,0:T(8,128)}), f32[8,2,32,1024]{3,2,1,0:T(8,128)}) %all-reduce.9.cloned.1.call-update) | async-done | bytes 2097168
  (166 shorter events, 76.3 us)
Async XLA Ops:
  7.2 357.0 %copy-start = (bf16[8,2,32,1024]{3,2,1,0:T(8,128)(2,1)S(1)}, bf16[8,2,32,1024]{3,2,1,0:T(8,128)(2,1)}, u32[]{:S(2)}) copy-start(bf16[8,2,32,1024]{3,2,1,0:T(8,128)(2,1)} %param.12) | copy-start | bytes 3145732
  7.2 125.2 %all-reduce.5.cloned.1.call-start = ((), (), s32[]{:S(2)}) async-start(), calls=%async_computation | async-start | bytes 786432 | tf_op jit(solution)/shard_map/psum | solution.py:67
  11.9 6.4 %copy-start.12 = (f32[32,32]{0,1:T(8,128)S(1)}, f32[32,32]{0,1:T(8,128)}, u32[]{:S(2)}) copy-start(f32[32,32]{0,1:T(8,128)} %constant.158.clone.1) | copy-start | bytes 12292
  48.5 20.7 %copy-start.1 = (f32[8,32,32,32]{3,2,1,0:T(8,128)S(1)}, f32[8,32,32,32]{3,2,1,0:T(8,128)}, u32[]{:S(2)}) copy-start(f32[8,32,32,32]{3,2,1,0:T(8,128)} %reshape.220) | copy-start | bytes 3145732
  82.9 9.8 %copy-start.5 = (f32[8,32,32,32]{2,1,3,0:T(8,128)S(1)}, f32[8,32,32,32]{2,1,3,0:T(8,128)}, u32[]{:S(2)}) copy-start(f32[8,32,32,32]{2,1,3,0:T(8,128)} %copy.94) | copy-start | bytes 3145732
  82.9 9.8 %copy-start.9 = (f32[8,32,32,32]{2,1,3,0:T(8,128)S(1)}, f32[8,32,32,32]{2,1,3,0:T(8,128)}, u32[]{:S(2)}) copy-start(f32[8,32,32,32]{2,1,3,0:T(8,128)} %copy.93) | copy-start | bytes 3145732
  96.8 6.3 %copy-start.2 = (f32[8,32,32,32]{3,2,1,0:T(8,128)S(1)}, f32[8,32,32,32]{3,2,1,0:T(8,128)}, u32[]{:S(2)}) copy-start(f32[8,32,32,32]{3,2,1,0:T(8,128)} %reshape.220) | copy-start | bytes 3145732
  103.1 8.2 %copy-start.13 = (s32[8,3]{0,1:T(4,128)S(1)}, s32[8,3]{0,1:T(4,128)}, u32[]{:S(2)}) copy-start(s32[8,3]{0,1:T(4,128)} %param.14) | copy-start | bytes 292
  103.2 8.2 %copy-start.10 = (f32[8,1,32,1024]{3,2,1,0:T(8,128)S(1)}, f32[8,1,32,1024]{3,2,1,0:T(8,128)}, u32[]{:S(2)}) copy-start(f32[8,1,32,1024]{3,2,1,0:T(8,128)} %param.11) | copy-start | bytes 3145732
  111.0 183.7 %all-reduce.7.cloned.1.call-start = ((), (), s32[]{:S(2)}) async-start(), calls=%async_computation.1 | async-start | bytes 786432 | tf_op jit(solution)/shard_map/psum | solution.py:67
  114.1 72.9 %copy-start.11 = (f32[1,1024]{1,0:T(1,128)S(1)}, f32[1,1024]{1,0:T(1,128)}, u32[]{:S(2)}) copy-start(f32[1,1024]{1,0:T(1,128)} %constant.167.clone.1) | copy-start | bytes 12292
  217.7 20.9 %copy-start.3 = (f32[8,32,32,32]{3,2,1,0:T(8,128)S(1)}, f32[8,32,32,32]{3,2,1,0:T(8,128)}, u32[]{:S(2)}) copy-start(f32[8,32,32,32]{3,2,1,0:T(8,128)} %reshape.220) | copy-start | bytes 3145732
  238.6 6.9 %copy-start.6 = (f32[8,32,32,32]{2,1,3,0:T(8,128)S(1)}, f32[8,32,32,32]{2,1,3,0:T(8,128)}, u32[]{:S(2)}) copy-start(f32[8,32,32,32]{2,1,3,0:T(8,128)} %copy.94) | copy-start | bytes 3145732
  258.3 7.7 %copy-start.7 = (f32[8,32,32,32]{3,1,2,0:T(8,128)S(1)}, f32[8,32,32,32]{3,1,2,0:T(8,128)}, u32[]{:S(2)}) copy-start(f32[8,32,32,32]{3,1,2,0:T(8,128)} %fusion.18) | copy-start | bytes 3145732
  266.0 6.2 %copy-start.4 = (f32[8,32,32,32]{3,2,1,0:T(8,128)S(1)}, f32[8,32,32,32]{3,2,1,0:T(8,128)}, u32[]{:S(2)}) copy-start(f32[8,32,32,32]{3,2,1,0:T(8,128)} %reshape.220) | copy-start | bytes 3145732
  280.2 208.1 %all-reduce.9.cloned.1.call-start = ((), (), s32[]{:S(2)}) async-start(), calls=%async_computation.2 | async-start | bytes 4194304
  367.9 7.6 %collective-permute-start = (bf16[2,4096]{1,0:T(2,128)(2,1)S(1)}, bf16[2,4096]{1,0:T(2,128)(2,1)S(1)}, u32[]{:S(2)}, u32[]{:S(2)}) collective-permute-start(bf16[2,4096]{1,0:T(2,128)(2,1)S(1)} %gather_fusion.6), channel_id=1, source_target_pairs={{0,2},{2,4},{4,6},{6,8},{8,10},{10,12},{12,14},{14,16},{16,18},{18... | collective-permute-start | bytes 49160 | tf_op jit(solution)/shard_map/ppermute | solution.py:101
  368.2 7.3 %collective-permute-start.1 = (bf16[2,4096]{1,0:T(2,128)(2,1)S(1)}, bf16[2,4096]{1,0:T(2,128)(2,1)S(1)}, u32[]{:S(2)}, u32[]{:S(2)}) collective-permute-start(bf16[2,4096]{1,0:T(2,128)(2,1)S(1)} %gather_fusion.6), channel_id=1, source_target_pairs={{0,30},{2,0},{4,2},{6,4},{8,6},{10,8},{12,10},{14,12},{16,14},{18,... | collective-permute-start | bytes 49160 | tf_op jit(solution)/shard_map/ppermute | solution.py:109
  375.5 7.3 %collective-permute-start.2 = (bf16[2,4096]{1,0:T(2,128)(2,1)S(1)}, bf16[2,4096]{1,0:T(2,128)(2,1)S(1)}, u32[]{:S(2)}, u32[]{:S(2)}) collective-permute-start(bf16[2,4096]{1,0:T(2,128)(2,1)S(1)} %collective-permute-done), channel_id=1, source_target_pairs={{0,2},{2,4},{4,6},{6,8},{8,10},{10,12},{12,14},{14,16},{16,18},{18... | collective-permute-start | bytes 49160 | tf_op jit(solution)/shard_map/ppermute | solution.py:101
  375.6 7.3 %collective-permute-start.3 = (bf16[2,4096]{1,0:T(2,128)(2,1)S(1)}, bf16[2,4096]{1,0:T(2,128)(2,1)S(1)}, u32[]{:S(2)}, u32[]{:S(2)}) collective-permute-start(bf16[2,4096]{1,0:T(2,128)(2,1)S(1)} %collective-permute-done.1), channel_id=1, source_target_pairs={{0,30},{2,0},{4,2},{6,4},{8,6},{10,8},{12,10},{14,12},{16,14},{18,... | collective-permute-start | bytes 49160 | tf_op jit(solution)/shard_map/ppermute | solution.py:109
  382.9 7.3 %collective-permute-start.4 = (bf16[2,4096]{1,0:T(2,128)(2,1)S(1)}, bf16[2,4096]{1,0:T(2,128)(2,1)S(1)}, u32[]{:S(2)}, u32[]{:S(2)}) collective-permute-start(bf16[2,4096]{1,0:T(2,128)(2,1)S(1)} %collective-permute-done.2), channel_id=1, source_target_pairs={{0,2},{2,4},{4,6},{6,8},{8,10},{10,12},{12,14},{14,16},{16,18},{18... | collective-permute-start | bytes 49160 | tf_op jit(solution)/shard_map/ppermute | solution.py:101
  382.9 7.3 %collective-permute-start.5 = (bf16[2,4096]{1,0:T(2,128)(2,1)S(1)}, bf16[2,4096]{1,0:T(2,128)(2,1)S(1)}, u32[]{:S(2)}, u32[]{:S(2)}) collective-permute-start(bf16[2,4096]{1,0:T(2,128)(2,1)S(1)} %collective-permute-done.3), channel_id=1, source_target_pairs={{0,30},{2,0},{4,2},{6,4},{8,6},{10,8},{12,10},{14,12},{16,14},{18,... | collective-permute-start | bytes 49160 | tf_op jit(solution)/shard_map/ppermute | solution.py:109
  390.2 7.3 %collective-permute-start.6 = (bf16[2,4096]{1,0:T(2,128)(2,1)S(1)}, bf16[2,4096]{1,0:T(2,128)(2,1)S(1)}, u32[]{:S(2)}, u32[]{:S(2)}) collective-permute-start(bf16[2,4096]{1,0:T(2,128)(2,1)S(1)} %collective-permute-done.4), channel_id=1, source_target_pairs={{0,2},{2,4},{4,6},{6,8},{8,10},{10,12},{12,14},{14,16},{16,18},{18... | collective-permute-start | bytes 49160 | tf_op jit(solution)/shard_map/ppermute | solution.py:101
  390.2 7.3 %collective-permute-start.7 = (bf16[2,4096]{1,0:T(2,128)(2,1)S(1)}, bf16[2,4096]{1,0:T(2,128)(2,1)S(1)}, u32[]{:S(2)}, u32[]{:S(2)}) collective-permute-start(bf16[2,4096]{1,0:T(2,128)(2,1)S(1)} %collective-permute-done.5), channel_id=1, source_target_pairs={{0,30},{2,0},{4,2},{6,4},{8,6},{10,8},{12,10},{14,12},{16,14},{18,... | collective-permute-start | bytes 49160 | tf_op jit(solution)/shard_map/ppermute | solution.py:109
  397.6 7.3 %collective-permute-start.8 = (bf16[2,4096]{1,0:T(2,128)(2,1)S(1)}, bf16[2,4096]{1,0:T(2,128)(2,1)S(1)}, u32[]{:S(2)}, u32[]{:S(2)}) collective-permute-start(bf16[2,4096]{1,0:T(2,128)(2,1)S(1)} %collective-permute-done.6), channel_id=1, source_target_pairs={{0,2},{2,4},{4,6},{6,8},{8,10},{10,12},{12,14},{14,16},{16,18},{18... | collective-permute-start | bytes 49160 | tf_op jit(solution)/shard_map/ppermute | solution.py:101
  397.6 7.3 %collective-permute-start.9 = (bf16[2,4096]{1,0:T(2,128)(2,1)S(1)}, bf16[2,4096]{1,0:T(2,128)(2,1)S(1)}, u32[]{:S(2)}, u32[]{:S(2)}) collective-permute-start(bf16[2,4096]{1,0:T(2,128)(2,1)S(1)} %collective-permute-done.7), channel_id=1, source_target_pairs={{0,30},{2,0},{4,2},{6,4},{8,6},{10,8},{12,10},{14,12},{16,14},{18,... | collective-permute-start | bytes 49160 | tf_op jit(solution)/shard_map/ppermute | solution.py:109
  404.9 7.3 %collective-permute-start.10 = (bf16[2,4096]{1,0:T(2,128)(2,1)S(1)}, bf16[2,4096]{1,0:T(2,128)(2,1)S(1)}, u32[]{:S(2)}, u32[]{:S(2)}) collective-permute-start(bf16[2,4096]{1,0:T(2,128)(2,1)S(1)} %collective-permute-done.8), channel_id=1, source_target_pairs={{0,2},{2,4},{4,6},{6,8},{8,10},{10,12},{12,14},{14,16},{16,18},{18... | collective-permute-start | bytes 49160 | tf_op jit(solution)/shard_map/ppermute | solution.py:101
  404.9 7.3 %collective-permute-start.11 = (bf16[2,4096]{1,0:T(2,128)(2,1)S(1)}, bf16[2,4096]{1,0:T(2,128)(2,1)S(1)}, u32[]{:S(2)}, u32[]{:S(2)}) collective-permute-start(bf16[2,4096]{1,0:T(2,128)(2,1)S(1)} %collective-permute-done.9), channel_id=1, source_target_pairs={{0,30},{2,0},{4,2},{6,4},{8,6},{10,8},{12,10},{14,12},{16,14},{18,... | collective-permute-start | bytes 49160 | tf_op jit(solution)/shard_map/ppermute | solution.py:109
  412.2 7.3 %collective-permute-start.12 = (bf16[2,4096]{1,0:T(2,128)(2,1)S(1)}, bf16[2,4096]{1,0:T(2,128)(2,1)S(1)}, u32[]{:S(2)}, u32[]{:S(2)}) collective-permute-start(bf16[2,4096]{1,0:T(2,128)(2,1)S(1)} %collective-permute-done.10), channel_id=1, source_target_pairs={{0,2},{2,4},{4,6},{6,8},{8,10},{10,12},{12,14},{14,16},{16,18},{18... | collective-permute-start | bytes 49160 | tf_op jit(solution)/shard_map/ppermute | solution.py:101
  412.2 7.4 %collective-permute-start.13 = (bf16[2,4096]{1,0:T(2,128)(2,1)S(1)}, bf16[2,4096]{1,0:T(2,128)(2,1)S(1)}, u32[]{:S(2)}, u32[]{:S(2)}) collective-permute-start(bf16[2,4096]{1,0:T(2,128)(2,1)S(1)} %collective-permute-done.11), channel_id=1, source_target_pairs={{0,30},{2,0},{4,2},{6,4},{8,6},{10,8},{12,10},{14,12},{16,14},{18,... | collective-permute-start | bytes 49160 | tf_op jit(solution)/shard_map/ppermute | solution.py:109
  419.6 7.3 %collective-permute-start.14 = (bf16[2,4096]{1,0:T(2,128)(2,1)S(1)}, bf16[2,4096]{1,0:T(2,128)(2,1)S(1)}, u32[]{:S(2)}, u32[]{:S(2)}) collective-permute-start(bf16[2,4096]{1,0:T(2,128)(2,1)S(1)} %collective-permute-done.12), channel_id=1, source_target_pairs={{0,2},{2,4},{4,6},{6,8},{8,10},{10,12},{12,14},{14,16},{16,18},{18... | collective-permute-start | bytes 49160 | tf_op jit(solution)/shard_map/ppermute | solution.py:101
  463.3 7.8 %copy-start.20 = (u32[32]{0:T(128)S(1)}, u32[32]{0:T(128)}, u32[]{:S(2)}) copy-start(u32[32]{0:T(128)} %constant.199) | copy-start | bytes 388
  (7 other events, 29.0 us)
Sparse Core Ops, SparseCore 0:
  111.1 21.1 all-reduce.4
  280.3 14.3 all-reduce.6
  471.2 17.0 all-reduce.8
